TPU v7x, 512 devices: a whole 4x4x16 slice. The times are simulated.
512 devices in a mesh: chol: 8 (over x, core), ao: 64 (over z, y).
Axes of the slice: x: 4, y: 4, z: 16, core: 2. Of those that a mesh axis runs over, the one named last changes fastest.
Arguments:
- cholesky: bfloat16 [32, 4096, 4096], P('chol', 'ao'), may hold values from -6 to 6
- orbitals: bfloat16 [4096, 256], replicated, may hold values from -0.09375 to 0.09375
- tile_pairs: int32 [64, 4, 2], P('ao'), may hold values from 0 to 255, as said below
Outputs:
- integrals: float32 [256, 256, 256], P('ao', 'chol')
Inputs may be any that keep to these rules, and one draw needn't show every extreme that they name: `tile_pairs`: each pair has p <= r; every index of ao has 4 tiles.
All inputs are finite; a program needn't handle non-finite values.
Results may differ from a plain program's by a relative error of at most 0.0057.
Values may be sent and summed in bfloat16 or wider, within the bound.
A program may use at most 64 MiB of HBM per device.

v0:
```python
import jax
import jax.numpy as jnp
from jax import lax
from jax.sharding import PartitionSpec as P


def on_device(cholesky, orbitals, tile_pairs):
    atomic_orbital_rows = cholesky.shape[1]
    half = jnp.einsum("cmn,np->cmp", cholesky, orbitals, preferred_element_type=jnp.float32).astype(
        jnp.bfloat16
    )
    mine = lax.dynamic_slice_in_dim(
        orbitals, lax.axis_index("ao") * atomic_orbital_rows, atomic_orbital_rows, 0
    )
    owned = lax.psum_scatter(
        jnp.einsum("mp,cmq->pcq", mine, half, preferred_element_type=jnp.float32),
        "ao",
        scatter_dimension=0,
        tiled=True,
    ).astype(jnp.bfloat16)
    every = lax.all_gather(owned, "ao", axis=0, tiled=True)
    entries = tile_pairs[0]
    left_factor = jnp.take(every, entries[:, 0], axis=0)
    right_factor = jnp.take(every, entries[:, 1], axis=0)
    contraction_terms = jnp.einsum(
        "wez,wed->wzd", left_factor, right_factor, preferred_element_type=jnp.float32
    )
    result = lax.psum_scatter(contraction_terms, "chol", scatter_dimension=1, tiled=True)
    return result


def solution(mesh):
    return jax.shard_map(
        on_device,
        mesh=mesh,
        in_specs=(P("chol", "ao", None), P(), P("ao", None, None)),
        out_specs=P("ao", "chol", None),
        check_vma=False,
    )
```

profile of v0, /device:TPU:1, one launch (start us, length us, event | category | flops | bytes accessed | tf_op | source)
XLA Modules:
  0.0 449.0 jit_solution(17293737828018765265)
XLA Ops:
  6.5 0.0 copy-start
  6.5 0.0 reduce-scatter.3.cloned.1.call-start
  6.5 1.6 copy-done
  8.1 2.8 fusion.6
  11.0 0.0 copy-start.1
  11.0 241.4 %all-reduce.2 = bf16[256,4,256]{2,0,1:T(8,128)(2,1)} all-reduce(f32[256,4,256]{2,0,1:T(8,128)S(1)} %fusion.6), channel_id=2, replica_groups=mesh['chol'=8,'ao'=64] {'ao'}, use_global_device_ids=true, to_apply=%region_0.0.clone | all-reduce | flops 262144 | bytes 1572864
  252.4 1.3 dynamic-slice
  254.3 0.7 dynamic-slice_convert_fusion
  255.0 71.6 %all_gather.3 = bf16[256,4,256]{2,1,0:T(4,128)(2,1)S(1)} all-gather(bf16[4,4,256]{2,1,0:T(4,128)(2,1)S(1)} %copy.8), channel_id=1, replica_groups=mesh['chol'=8,'ao'=64] {'ao'}, dimensions={0}, use_global_device_ids=true | all-gather | bytes 532480 | tf_op jit(solution)/shard_map/all_gather | solution.py:21
  326.6 0.0 copy-done.1
  326.7 0.6 gather_fusion
  327.2 0.6 gather_fusion.1
  327.8 1.4 fusion.10
  329.2 0.0 reduce-scatter.3.cloned.1.call-update
  329.2 112.9 %reduce-scatter.3.cloned.1.call-done = f32[4,32,256]{2,1,0:T(8,128)} async-done(((f32[4,256,256]{2,1,0:T(8,128)}), f32[4,32,256]{2,1,0:T(8,128)}) %reduce-scatter.3.cloned.1.call-update) | async-done | bytes 131088 | tf_op jit(solution)/shard_map/reduce_scatter | solution.py:28
  (3 shorter events, 0.0 us)
Async XLA Ops:
  6.5 1.6 copy-start
  6.5 435.6 %reduce-scatter.3.cloned.1.call-start = ((), (), s32[]{:S(2)}) async-start(), calls=%async_computation.1 | async-start | bytes 1179648 | tf_op jit(solution)/shard_map/reduce_scatter | solution.py:28
  11.0 315.7 %copy-start.1 = (s32[1,4,2]{1,2,0:T(2,128)S(1)}, s32[1,4,2]{1,2,0:T(2,128)}, u32[]{:S(2)}) copy-start(s32[1,4,2]{1,2,0:T(2,128)} %param.7) | copy-start | bytes 100
Sparse Core Ops, SparseCore 0:
  329.4 112.7 reduce-scatter.2
where the time goes:
time: 450 us; the launch traced here: 449 us
  blocking collectives  313 us (70%)
  waiting for transfers between devices  113 us (25%)
  between operations  14.1 us (3%)
  local copies, waits for them, and re-layouts  4.74 us (1%)
    unnamed x1, blocking collectives  241 us
    reduce_scatter x1, waiting for transfers between devices, on_device(): lax.psum_scatter(contraction_terms, 'chol', scatter_dimension=1, tiled=True)  113 us
    all_gather x1, blocking collectives, on_device(): every = lax.all_gather(owned, 'ao', axis=0, tiled=True)  71.6 us
  transfers between devices with their start and end apart: 1, of which 1 were waited for; matrix products, arithmetic and copies ran while one was open for 0% of the time, Pallas kernels for 0%

commit v1 on v0

v1 whole, which is shorter than its diff:
```python
import jax
import jax.numpy as jnp
from jax import lax
from jax.experimental import pallas as pl
from jax.experimental.pallas import tpu as pltpu
from jax.sharding import PartitionSpec as P

MESH = pl.DeviceIdType.MESH
BF16, F32 = jnp.bfloat16, jnp.float32
GROUP = 16
QUADS = 4
CHOL = 8
CHUNKS = 4


def kernel(chol_hbm, orb_hbm, pairs_hbm, out_ref, chol_v, orb_v, pairs_s, acc, half_send, half_recv, orb_t,
           part_send, part_recv, index_send, index_recv, rows_send, rows_recv,
           load_sem, pairs_sem, half_sems, part_sems, index_sems, rows_sems):
    c, a = lax.axis_index("chol"), lax.axis_index("ao")
    quad, i = a // GROUP, a % GROUP
    base = quad * GROUP
    y, zl = i % 4, i // 4
    width = chol_v.shape[2] // CHUNKS

    loads = []
    for j in range(CHUNKS):
        cols = pl.ds(j * width, width)
        pair = (
            pltpu.make_async_copy(chol_hbm.at[:, :, cols], chol_v.at[:, :, cols], load_sem.at[0, j]),
            pltpu.make_async_copy(orb_hbm.at[cols, :], orb_v.at[cols, :], load_sem.at[1, j]),
        )
        for copy in pair:
            copy.start()
        loads.append(pair)
    pairs_copy = pltpu.make_async_copy(pairs_hbm, pairs_s, pairs_sem)
    pairs_copy.start()

    barrier = pltpu.get_barrier_semaphore()
    for d in range(1, QUADS):
        pl.semaphore_signal(barrier, 1, device_id=(c, (a + GROUP * d) % 64), device_id_type=MESH)
    for d in range(1, GROUP):
        pl.semaphore_signal(barrier, 1, device_id=(c, base + (i ^ d)), device_id_type=MESH)
    for d in range(1, CHOL):
        pl.semaphore_signal(barrier, 1, device_id=(c ^ d, a), device_id_type=MESH)

    lane = lambda rows: lax.broadcasted_iota(jnp.int32, (rows, 128), 1)
    row = lambda rows: lax.broadcasted_iota(jnp.int32, (rows, 128), 0)
    swap = lambda v: pltpu.roll(v, 64, axis=1)

    for j in range(CHUNKS):
        for copy in loads[j]:
            copy.wait()
        cols = pl.ds(j * width, width)
        term = jnp.dot(chol_v[:, :, cols].reshape(256, width), orb_v[cols, :], preferred_element_type=F32)
        acc[...] = term if j == 0 else acc[...] + term
    low32 = lane(32) < 64
    for k in range(4):
        for h in range(2):
            first = acc[k * 64 : k * 64 + 32, h * 128 : h * 128 + 128]
            second = acc[k * 64 + 32 : k * 64 + 64, h * 128 : h * 128 + 128]
            half_send[(2 * h) * 4 + k] = jnp.where(low32, first, swap(second)).astype(BF16)
            half_send[(2 * h + 1) * 4 + k] = jnp.where(low32, swap(first), second).astype(BF16)
    half_recv[i] = half_send[i]

    pairs_copy.wait()
    line = jnp.zeros((1, 128), F32)
    for t in range(4):
        for e in range(2):
            line = jnp.where(lane(1) == 2 * t + e, pairs_s[0, t, e].astype(F32), line)
    index_send[0] = line
    index_recv[i] = line

    pl.semaphore_wait(barrier, QUADS - 1 + GROUP - 1 + CHOL - 1)

    halves, indices = [], []
    for d in (10, 11, 9, 8, 14, 15, 13, 12, 6, 7, 5, 4, 2, 3, 1):
        to = (c, base + (i ^ d))
        halves.append(pltpu.make_async_remote_copy(
            half_send.at[i ^ d], half_recv.at[i], half_sems.at[0], half_sems.at[1], device_id=to, device_id_type=MESH))
        indices.append(pltpu.make_async_remote_copy(
            index_send.at[0], index_recv.at[i], index_sems.at[0], index_sems.at[1], device_id=to, device_id_type=MESH))
    for copy in halves:
        copy.start()
    for copy in indices:
        copy.start()

    eye = (lax.broadcasted_iota(jnp.int32, (256, 256), 0) == lax.broadcasted_iota(jnp.int32, (256, 256), 1)).astype(BF16)
    mine = orb_v[pl.ds(quad * 1024, 1024), :].reshape(16, 2, 32, 256)
    for h in range(2):
        orb_t[h] = lax.dot_general(
            eye, mine[:, h].reshape(512, 256), (((1,), (1,)), ((), ())), preferred_element_type=F32).astype(BF16)

    def wait_for(sem, ref):
        pltpu.make_async_copy(ref, ref, sem).wait()

    wait_for(half_sems.at[1], half_recv.at[pl.ds(0, GROUP - 1)])

    block = half_recv[...].reshape(512, 128)
    even = jnp.dot(orb_t[0], block, preferred_element_type=F32)
    odd = jnp.dot(orb_t[1], block, preferred_element_type=F32)
    own = jnp.where(lane(128) < 64, even[:128] + swap(odd[:128]), swap(even[128:]) + odd[128:])
    part_send[...] = own.astype(BF16)
    parts = []
    for d in (2, 1, 3):
        copy = pltpu.make_async_remote_copy(
            part_send, part_recv.at[d - 1], part_sems.at[0], part_sems.at[d],
            device_id=(c, (a + GROUP * d) % 64), device_id_type=MESH)
        copy.start()
        parts.append(copy)
    acc[:128, :128] = own

    wait_for(index_sems.at[1], index_recv.at[pl.ds(0, GROUP - 1)])
    table = jnp.broadcast_to(index_recv[...], (16, 4, 128)).reshape(64, 128)
    picks = []
    for e in range(2):
        column = jnp.sum(jnp.where(lane(64) == 2 * (row(64) % 4) + e, table, 0.0), axis=1, keepdims=True)
        picks.append(column.astype(jnp.int32))
    hot = lambda e, h: (picks[e] - 128 * h == lane(64)).astype(BF16)
    ones = jnp.concatenate([hot(0, 0), hot(1, 0), hot(0, 1), hot(1, 1)], axis=0)

    total = acc[:128, :128]
    for copy in parts:
        copy.wait_recv()
    for d in range(3):
        total = total + part_recv[d].astype(F32)
    chosen = jnp.dot(ones, total.astype(BF16), preferred_element_type=F32)
    message = jnp.where(
        lane(64) < 64, chosen[:64] + swap(chosen[128:192]), swap(chosen[64:128]) + chosen[192:256])
    rows_send[...] = message.reshape(16, 4, 128)
    slot = zl * 32 + y * 8 + c
    rows_recv[slot] = rows_send[i]

    def send(j, carry):
        d = 127 - j
        pltpu.make_async_remote_copy(
            rows_send.at[i ^ (d // 8)], rows_recv.at[slot], rows_sems.at[0], rows_sems.at[1],
            device_id=(c ^ (d % 8), base + (i ^ (d // 8))), device_id_type=MESH).start()
        return carry

    lax.fori_loop(0, 127, send, 0)
    for copy in parts:
        copy.wait_send()
    for copy in indices:
        copy.wait_send()
    wait_for(half_sems.at[0], half_recv.at[pl.ds(0, GROUP - 1)])
    wait_for(rows_sems.at[1], rows_recv.at[pl.ds(0, 127)])

    left = rows_recv[pl.ds((c // 2) * 32, 32)].reshape(128, 128)
    left = jnp.where(c % 2 == 0, left, pltpu.roll(left, 96, axis=1))
    wide = jnp.zeros((128, 128), F32)
    for t in range(4):
        moved = left if t == 0 else pltpu.roll(left, 32 * t, axis=1)
        wide = jnp.where((row(128) % 4 == t) & (lane(128) // 32 == t), moved, wide)
    wide = wide.astype(BF16)
    products = [
        lax.dot_general(wide, rows_recv[z * 32 : z * 32 + 32].reshape(128, 128).astype(BF16),
                        (((0,), (0,)), ((), ())), preferred_element_type=F32)
        for z in range(4)
    ]
    for h in range(2):
        joined = jnp.where(lane(128) < 64, swap(products[2 * h]), products[2 * h + 1])
        out_ref[:, :, h * 128 : h * 128 + 128] = joined.reshape(4, 32, 128)
    wait_for(rows_sems.at[0], rows_recv.at[pl.ds(0, 127)])


def on_device(cholesky, orbitals, tile_pairs):
    vmem, dma = pltpu.VMEM, pltpu.SemaphoreType.DMA
    return pl.pallas_call(
        kernel,
        out_shape=jax.ShapeDtypeStruct((4, 32, 256), F32),
        in_specs=[pl.BlockSpec(memory_space=pl.ANY)] * 3,
        out_specs=pl.BlockSpec(memory_space=pltpu.VMEM),
        scratch_shapes=[
            vmem(cholesky.shape, BF16),
            vmem(orbitals.shape, BF16),
            pltpu.SMEM(tile_pairs.shape, jnp.int32),
            vmem((256, 256), F32),
            vmem((16, 32, 128), BF16),
            vmem((16, 32, 128), BF16),
            vmem((2, 256, 512), BF16),
            vmem((128, 128), BF16),
            vmem((3, 128, 128), BF16),
            vmem((1, 1, 128), F32),
            vmem((16, 1, 128), F32),
            vmem((16, 4, 128), F32),
            vmem((128, 4, 128), F32),
            dma((2, CHUNKS)),
            dma,
            dma((2,)),
            dma((4,)),
            dma((2,)),
            dma((2,)),
        ],
        compiler_params=pltpu.CompilerParams(
            collective_id=0, has_side_effects=True, vmem_limit_bytes=48 * 2**20),
        cost_estimate=pl.CostEstimate(flops=700_000_000, bytes_accessed=4_400_000, transcendentals=0),
    )(cholesky, orbitals, tile_pairs)


def solution(mesh):
    return jax.shard_map(
        on_device,
        mesh=mesh,
        in_specs=(P("chol", "ao", None), P(), P("ao", None, None)),
        out_specs=P("ao", "chol", None),
        check_vma=False,
    )
```

time: 450 us -> 45.2 us (0.10)
  blocking collectives: 313 us -> 0 us
  waiting for transfers between devices: 113 us -> 0 us
  Pallas kernels: 0 us -> 40.4 us
  between operations: 14.1 us -> 0.01 us
    unnamed x1 -> x0, blocking collectives: 241 us -> none
    reduce_scatter x1 -> x0, waiting for transfers between devices: 113 us -> none  [on_device(): lax.psum_scatter(contraction_terms, 'chol', scatter_dimension=1, tiled=True)]
    all_gather x1 -> x0, blocking collectives: 71.6 us -> none  [on_device(): every = lax.all_gather(owned, 'ao', axis=0, tiled=True)]
    pallas_call x0 -> x1, Pallas kernels: none -> 40.4 us  [on_device(): pl.pallas_call(kernel, out_shape=jax.ShapeDtypeStruct((4, 32, 256), F32),...]
  transfers between devices with their start and end apart: 1 -> 0, of which waited for: 1 -> 0; matrix products, arithmetic and copies ran while one was open for 0% -> 0% of each run, Pallas kernels for 0% -> 0%
where the time goes in v1:
time: 45.2 us; the launch traced here: 45 us
  Pallas kernels  40.4 us (89%)
  local copies, waits for them, and re-layouts  4.6 us (10%)
    pallas_call x1, Pallas kernels, on_device(): pl.pallas_call(kernel, out_shape=jax.ShapeDtypeStruct((4, 32, 256), F32),...  40.4 us
    unnamed x6, local copies, waits for them, and re-layouts  4.6 us

profile of v1, /device:TPU:1, one launch (start us, length us, event | category | flops | bytes accessed | tf_op | source)
XLA Modules:
  0.0 45.0 jit_solution(4063807062139341270)
XLA Ops:
  0.0 0.8 %copy.4.pairs_hbm = s32[1,4,2]{2,1,0:T(4,128)S(1)} copy(s32[1,4,2]{1,2,0:T(2,128)} %param.5) | data formatting | bytes 64 | tf_op args[2]
  0.8 0.0 copy-start
  0.8 1.6 %copy-done = bf16[4,64,4096]{2,1,0:T(8,128)(2,1)S(1)} copy-done((bf16[4,64,4096]{2,1,0:T(8,128)(2,1)S(1)}, bf16[4,64,4096]{2,1,0:T(8,128)(2,1)}, u32[]{:S(2)}) %copy-start) | copy-done | bytes 2097176
  2.4 0.0 copy-start.1
  2.4 1.6 %copy-done.1 = bf16[4096,256]{1,0:T(8,128)(2,1)S(1)} copy-done((bf16[4096,256]{1,0:T(8,128)(2,1)S(1)}, bf16[4096,256]{1,0:T(8,128)(2,1)}, u32[]{:S(2)}) %copy-start.1) | copy-done | bytes 2097176
  3.9 40.4 %shard_map.37 = f32[4,32,256]{2,1,0:T(8,128)S(1)} custom-call(bf16[4,64,4096]{2,1,0:T(8,128)(2,1)S(1)} %copy-done, bf16[4096,256]{1,0:T(8,128)(2,1)S(1)} %copy-done.1, s32[1,4,2]{2,1,0:T(4,128)S(1)} %copy.4.pairs_hbm), custom_call_target="tpu_custom_call" | custom-call | flops 700000000 | bytes 4400000 | tf_op jit(solution)/shard_map/pallas_call | solution.py:168
  44.3 0.7 %copy.6 = f32[4,32,256]{2,1,0:T(8,128)} copy(f32[4,32,256]{2,1,0:T(8,128)S(1)} %shard_map.37) | data formatting | bytes 262144
Async XLA Ops:
  0.8 1.6 %copy-start = (bf16[4,64,4096]{2,1,0:T(8,128)(2,1)S(1)}, bf16[4,64,4096]{2,1,0:T(8,128)(2,1)}, u32[]{:S(2)}) copy-start(bf16[4,64,4096]{2,1,0:T(8,128)(2,1)} %chol_hbm.1) | copy-start | bytes 6291460
  2.4 1.6 %copy-start.1 = (bf16[4096,256]{1,0:T(8,128)(2,1)S(1)}, bf16[4096,256]{1,0:T(8,128)(2,1)}, u32[]{:S(2)}) copy-start(bf16[4096,256]{1,0:T(8,128)(2,1)} %orb_hbm.1) | copy-start | bytes 6291460

commit v2 on v1

--- a/solution.py
+++ b/solution.py
@@ -11,15 +11,25 @@
 QUADS = 4
 CHOL = 8
 CHUNKS = 4
+SHIFT = 8
 
 
 def kernel(chol_hbm, orb_hbm, pairs_hbm, out_ref, chol_v, orb_v, pairs_s, acc, half_send, half_recv, orb_t,
            part_send, part_recv, index_send, index_recv, rows_send, rows_recv,
            load_sem, pairs_sem, half_sems, part_sems, index_sems, rows_sems):
     c, a = lax.axis_index("chol"), lax.axis_index("ao")
-    quad, i = a // GROUP, a % GROUP
-    base = quad * GROUP
-    y, zl = i % 4, i // 4
+    shifted = (a + SHIFT) & 63
+    quad, i = shifted >> 4, shifted & 15
+    flip = 12 * (quad >> 1)
+    block = i ^ flip
+
+    def member(place):
+        return (quad * GROUP + place - SHIFT) & 63
+
+    def same_block(d):
+        other = (quad + d) & 3
+        return (other * GROUP + (block ^ (12 * (other >> 1))) - SHIFT) & 63
+
     width = chol_v.shape[2] // CHUNKS
 
     loads = []
@@ -37,9 +47,9 @@
 
     barrier = pltpu.get_barrier_semaphore()
     for d in range(1, QUADS):
-        pl.semaphore_signal(barrier, 1, device_id=(c, (a + GROUP * d) % 64), device_id_type=MESH)
+        pl.semaphore_signal(barrier, 1, device_id=(c, same_block(d)), device_id_type=MESH)
     for d in range(1, GROUP):
-        pl.semaphore_signal(barrier, 1, device_id=(c, base + (i ^ d)), device_id_type=MESH)
+        pl.semaphore_signal(barrier, 1, device_id=(c, member(i ^ d)), device_id_type=MESH)
     for d in range(1, CHOL):
         pl.semaphore_signal(barrier, 1, device_id=(c ^ d, a), device_id_type=MESH)
 
@@ -60,13 +70,13 @@
             second = acc[k * 64 + 32 : k * 64 + 64, h * 128 : h * 128 + 128]
             half_send[(2 * h) * 4 + k] = jnp.where(low32, first, swap(second)).astype(BF16)
             half_send[(2 * h + 1) * 4 + k] = jnp.where(low32, swap(first), second).astype(BF16)
-    half_recv[i] = half_send[i]
+    half_recv[i] = half_send[block]
 
     pairs_copy.wait()
     line = jnp.zeros((1, 128), F32)
     for t in range(4):
         for e in range(2):
-            line = jnp.where(lane(1) == 2 * t + e, pairs_s[0, t, e].astype(F32), line)
+            line = jnp.where(lane(1) == 2 * t + e, pairs_s[0, e, t].astype(F32), line)
     index_send[0] = line
     index_recv[i] = line
 
@@ -74,37 +84,37 @@
 
     halves, indices = [], []
     for d in (10, 11, 9, 8, 14, 15, 13, 12, 6, 7, 5, 4, 2, 3, 1):
-        to = (c, base + (i ^ d))
+        to = (c, member(i ^ d))
         halves.append(pltpu.make_async_remote_copy(
-            half_send.at[i ^ d], half_recv.at[i], half_sems.at[0], half_sems.at[1], device_id=to, device_id_type=MESH))
+            half_send.at[block ^ d], half_recv.at[i], half_sems.at[0], half_sems.at[1], device_id=to, device_id_type=MESH))
         indices.append(pltpu.make_async_remote_copy(
             index_send.at[0], index_recv.at[i], index_sems.at[0], index_sems.at[1], device_id=to, device_id_type=MESH))
-    for copy in halves:
+    for copy in halves + indices:
         copy.start()
-    for copy in indices:
-        copy.start()
 
     eye = (lax.broadcasted_iota(jnp.int32, (256, 256), 0) == lax.broadcasted_iota(jnp.int32, (256, 256), 1)).astype(BF16)
-    mine = orb_v[pl.ds(quad * 1024, 1024), :].reshape(16, 2, 32, 256)
-    for h in range(2):
-        orb_t[h] = lax.dot_general(
-            eye, mine[:, h].reshape(512, 256), (((1,), (1,)), ((), ())), preferred_element_type=F32).astype(BF16)
+    for z in range(4):
+        start = ((quad * GROUP + 4 * z - SHIFT) & 63) * 64
+        mine = orb_v[pl.ds(pl.multiple_of(start, 256), 256), :].reshape(4, 2, 32, 256)
+        for h in range(2):
+            orb_t[h, :, z * 128 : z * 128 + 128] = lax.dot_general(
+                eye, mine[:, h].reshape(128, 256), (((1,), (1,)), ((), ())), preferred_element_type=F32).astype(BF16)
 
     def wait_for(sem, ref):
         pltpu.make_async_copy(ref, ref, sem).wait()
 
     wait_for(half_sems.at[1], half_recv.at[pl.ds(0, GROUP - 1)])
 
-    block = half_recv[...].reshape(512, 128)
-    even = jnp.dot(orb_t[0], block, preferred_element_type=F32)
-    odd = jnp.dot(orb_t[1], block, preferred_element_type=F32)
+    rows = half_recv[...].reshape(512, 128)
+    even = jnp.dot(orb_t[0], rows, preferred_element_type=F32)
+    odd = jnp.dot(orb_t[1], rows, preferred_element_type=F32)
     own = jnp.where(lane(128) < 64, even[:128] + swap(odd[:128]), swap(even[128:]) + odd[128:])
     part_send[...] = own.astype(BF16)
     parts = []
     for d in (2, 1, 3):
         copy = pltpu.make_async_remote_copy(
             part_send, part_recv.at[d - 1], part_sems.at[0], part_sems.at[d],
-            device_id=(c, (a + GROUP * d) % 64), device_id_type=MESH)
+            device_id=(c, same_block(d)), device_id_type=MESH)
         copy.start()
         parts.append(copy)
     acc[:128, :128] = own
@@ -126,18 +136,23 @@
     chosen = jnp.dot(ones, total.astype(BF16), preferred_element_type=F32)
     message = jnp.where(
         lane(64) < 64, chosen[:64] + swap(chosen[128:192]), swap(chosen[64:128]) + chosen[192:256])
-    rows_send[...] = message.reshape(16, 4, 128)
-    slot = zl * 32 + y * 8 + c
+    rows_send[...] = message.astype(BF16).reshape(16, 4, 128)
+    slot = block * 8 + c
     rows_recv[slot] = rows_send[i]
 
-    def send(j, carry):
-        d = 127 - j
+    def send(place, f):
         pltpu.make_async_remote_copy(
-            rows_send.at[i ^ (d // 8)], rows_recv.at[slot], rows_sems.at[0], rows_sems.at[1],
-            device_id=(c ^ (d % 8), base + (i ^ (d // 8))), device_id_type=MESH).start()
+            rows_send.at[place], rows_recv.at[slot], rows_sems.at[0], rows_sems.at[1],
+            device_id=(c ^ f, member(place)), device_id_type=MESH).start()
+
+    def send_member(j, carry):
+        for f in (4, 5, 6, 7, 2, 3, 0, 1):
+            send(i ^ (15 - j), f)
         return carry
 
-    lax.fori_loop(0, 127, send, 0)
+    lax.fori_loop(0, 15, send_member, 0)
+    for f in (4, 5, 6, 7, 2, 3, 1):
+        send(i, f)
     for copy in parts:
         copy.wait_send()
     for copy in indices:
@@ -145,15 +160,15 @@
     wait_for(half_sems.at[0], half_recv.at[pl.ds(0, GROUP - 1)])
     wait_for(rows_sems.at[1], rows_recv.at[pl.ds(0, 127)])
 
-    left = rows_recv[pl.ds((c // 2) * 32, 32)].reshape(128, 128)
-    left = jnp.where(c % 2 == 0, left, pltpu.roll(left, 96, axis=1))
+    left = rows_recv[pl.ds((c >> 1) * 32, 32)].reshape(128, 128).astype(F32)
+    left = jnp.where((c & 1) == 0, left, pltpu.roll(left, 96, axis=1))
     wide = jnp.zeros((128, 128), F32)
     for t in range(4):
         moved = left if t == 0 else pltpu.roll(left, 32 * t, axis=1)
         wide = jnp.where((row(128) % 4 == t) & (lane(128) // 32 == t), moved, wide)
     wide = wide.astype(BF16)
     products = [
-        lax.dot_general(wide, rows_recv[z * 32 : z * 32 + 32].reshape(128, 128).astype(BF16),
+        lax.dot_general(wide, rows_recv[z * 32 : z * 32 + 32].reshape(128, 128),
                         (((0,), (0,)), ((), ())), preferred_element_type=F32)
         for z in range(4)
     ]
@@ -168,12 +183,12 @@
     return pl.pallas_call(
         kernel,
         out_shape=jax.ShapeDtypeStruct((4, 32, 256), F32),
-        in_specs=[pl.BlockSpec(memory_space=pl.ANY)] * 3,
+        in_specs=[pl.BlockSpec(memory_space=pltpu.HBM)] * 3,
         out_specs=pl.BlockSpec(memory_space=pltpu.VMEM),
         scratch_shapes=[
             vmem(cholesky.shape, BF16),
             vmem(orbitals.shape, BF16),
-            pltpu.SMEM(tile_pairs.shape, jnp.int32),
+            pltpu.SMEM((1, 2, 4), jnp.int32),
             vmem((256, 256), F32),
             vmem((16, 32, 128), BF16),
             vmem((16, 32, 128), BF16),
@@ -182,8 +197,8 @@
             vmem((3, 128, 128), BF16),
             vmem((1, 1, 128), F32),
             vmem((16, 1, 128), F32),
-            vmem((16, 4, 128), F32),
-            vmem((128, 4, 128), F32),
+            vmem((16, 4, 128), BF16),
+            vmem((128, 4, 128), BF16),
             dma((2, CHUNKS)),
             dma,
             dma((2,)),
@@ -192,9 +207,9 @@
             dma((2,)),
         ],
         compiler_params=pltpu.CompilerParams(
-            collective_id=0, has_side_effects=True, vmem_limit_bytes=48 * 2**20),
+            collective_id=0, has_side_effects=True, vmem_limit_bytes=60 * 2**20),
         cost_estimate=pl.CostEstimate(flops=700_000_000, bytes_accessed=4_400_000, transcendentals=0),
-    )(cholesky, orbitals, tile_pairs)
+    )(cholesky, orbitals, jnp.swapaxes(tile_pairs, 1, 2))
 
 
 def solution(mesh):

time: 45.2 us -> 40.8 us (0.903)
  local copies, waits for them, and re-layouts: 4.6 us -> 1.57 us
  Pallas kernels: 40.4 us -> 39.1 us
    unnamed x6 -> x1, local copies, waits for them, and re-layouts: 4.6 us -> 1.57 us
    pallas_call x1, Pallas kernels: 40.4 us -> 39.1 us  [on_device(): pl.pallas_call(kernel, out_shape=jax.ShapeDtypeStruct((4, 32, 256), F32),...]
where the time goes in v2:
time: 40.8 us; the launch traced here: 40.6 us
  Pallas kernels  39.1 us (96%)
  local copies, waits for them, and re-layouts  1.57 us (4%)
    pallas_call x1, Pallas kernels, on_device(): pl.pallas_call(kernel, out_shape=jax.ShapeDtypeStruct((4, 32, 256), F32),...  39.1 us
    unnamed x1, local copies, waits for them, and re-layouts  1.57 us

profile of v2, /device:TPU:1, one launch (start us, length us, event | category | flops | bytes accessed | tf_op | source)
XLA Modules:
  0.0 40.6 jit_solution(1161299998682413401)
XLA Ops:
  0.0 39.1 %shard_map.37 = f32[4,32,256]{2,1,0:T(8,128)} custom-call(bf16[4,64,4096]{2,1,0:T(8,128)(2,1)} %chol_hbm.1, bf16[4096,256]{1,0:T(8,128)(2,1)} %orb_hbm.1, s32[1,2,4]{2,1,0:T(2,128)} %bitcast.1), custom_call_target="tpu_custom_call" | custom-call | flops 700000000 | bytes 4400000 | tf_op jit(solution)/shard_map/pallas_call | solution.py:183
  39.1 1.6 %copy.5 = f32[4,32,256]{2,1,0:T(8,128)} copy(f32[4,32,256]{2,1,0:T(8,128)} %shard_map.37) | data formatting | bytes 262144

commit v3 on v2

--- a/solution.py
+++ b/solution.py
@@ -11,26 +11,32 @@
 QUADS = 4
 CHOL = 8
 CHUNKS = 4
-SHIFT = 8
 
 
 def kernel(chol_hbm, orb_hbm, pairs_hbm, out_ref, chol_v, orb_v, pairs_s, acc, half_send, half_recv, orb_t,
            part_send, part_recv, index_send, index_recv, rows_send, rows_recv,
            load_sem, pairs_sem, half_sems, part_sems, index_sems, rows_sems):
     c, a = lax.axis_index("chol"), lax.axis_index("ao")
-    shifted = (a + SHIFT) & 63
-    quad, i = shifted >> 4, shifted & 15
+    quad, i = a >> 4, a & 15
     flip = 12 * (quad >> 1)
     block = i ^ flip
 
     def member(place):
-        return (quad * GROUP + place - SHIFT) & 63
+        return quad * GROUP + place
 
     def same_block(d):
         other = (quad + d) & 3
-        return (other * GROUP + (block ^ (12 * (other >> 1))) - SHIFT) & 63
+        return other * GROUP + (block ^ (12 * (other >> 1)))
 
     width = chol_v.shape[2] // CHUNKS
+
+    barrier = pltpu.get_barrier_semaphore()
+    for d in (2, 1, 3):
+        pl.semaphore_signal(barrier, 1, device_id=(c, same_block(d)), device_id_type=MESH)
+    for d in (10, 11, 9, 8, 14, 15, 13, 12, 6, 7, 5, 4, 2, 3, 1):
+        pl.semaphore_signal(barrier, 1, device_id=(c, member(i ^ d)), device_id_type=MESH)
+    for d in (4, 5, 6, 7, 2, 3, 1):
+        pl.semaphore_signal(barrier, 1, device_id=(c ^ d, a), device_id_type=MESH)
 
     loads = []
     for j in range(CHUNKS):
@@ -44,14 +50,6 @@
         loads.append(pair)
     pairs_copy = pltpu.make_async_copy(pairs_hbm, pairs_s, pairs_sem)
     pairs_copy.start()
-
-    barrier = pltpu.get_barrier_semaphore()
-    for d in range(1, QUADS):
-        pl.semaphore_signal(barrier, 1, device_id=(c, same_block(d)), device_id_type=MESH)
-    for d in range(1, GROUP):
-        pl.semaphore_signal(barrier, 1, device_id=(c, member(i ^ d)), device_id_type=MESH)
-    for d in range(1, CHOL):
-        pl.semaphore_signal(barrier, 1, device_id=(c ^ d, a), device_id_type=MESH)
 
     lane = lambda rows: lax.broadcasted_iota(jnp.int32, (rows, 128), 1)
     row = lambda rows: lax.broadcasted_iota(jnp.int32, (rows, 128), 0)
@@ -94,7 +92,7 @@
 
     eye = (lax.broadcasted_iota(jnp.int32, (256, 256), 0) == lax.broadcasted_iota(jnp.int32, (256, 256), 1)).astype(BF16)
     for z in range(4):
-        start = ((quad * GROUP + 4 * z - SHIFT) & 63) * 64
+        start = (quad * GROUP + 4 * z) * 64
         mine = orb_v[pl.ds(pl.multiple_of(start, 256), 256), :].reshape(4, 2, 32, 256)
         for h in range(2):
             orb_t[h, :, z * 128 : z * 128 + 128] = lax.dot_general(
@@ -207,9 +205,9 @@
             dma((2,)),
         ],
         compiler_params=pltpu.CompilerParams(
-            collective_id=0, has_side_effects=True, vmem_limit_bytes=60 * 2**20),
+            collective_id=0, has_side_effects=True, vmem_limit_bytes=53 * 2**20),
         cost_estimate=pl.CostEstimate(flops=700_000_000, bytes_accessed=4_400_000, transcendentals=0),
-    )(cholesky, orbitals, jnp.swapaxes(tile_pairs, 1, 2))
+    )(cholesky, orbitals, pltpu.with_memory_space_constraint(jnp.swapaxes(tile_pairs, 1, 2), pltpu.HBM))
 
 
 def solution(mesh):

time: 40.8 us -> 38 us (0.931)
  Pallas kernels: 39.1 us -> 37.2 us
  local copies, waits for them, and re-layouts: 1.57 us -> 0.66 us
    pallas_call x1, Pallas kernels: 39.1 us -> 37.2 us  [on_device(): pl.pallas_call(kernel, out_shape=jax.ShapeDtypeStruct((4, 32, 256), F32),...]
    unnamed x1, local copies, waits for them, and re-layouts: 1.57 us -> 0.66 us
where the time goes in v3:
time: 38 us; the launch traced here: 37.8 us
  Pallas kernels  37.2 us (98%)
  local copies, waits for them, and re-layouts  0.66 us (2%)
    pallas_call x1, Pallas kernels, on_device(): pl.pallas_call(kernel, out_shape=jax.ShapeDtypeStruct((4, 32, 256), F32),...  37.2 us

profile of v3, /device:TPU:1, one launch (start us, length us, event | category | flops | bytes accessed | tf_op | source)
XLA Modules:
  0.0 37.8 jit_solution(8700925433939951952)
XLA Ops:
  0.0 37.2 %shard_map.37 = f32[4,32,256]{2,1,0:T(8,128)S(1)} custom-call(bf16[4,64,4096]{2,1,0:T(8,128)(2,1)} %chol_hbm.1, bf16[4096,256]{1,0:T(8,128)(2,1)} %orb_hbm.1, s32[1,2,4]{2,1,0:T(2,128)} %bitcast.1), custom_call_target="tpu_custom_call" | custom-call | flops 700000000 | bytes 4400000 | tf_op jit(solution)/shard_map/pallas_call | solution.py:181
  37.2 0.7 %copy.5 = f32[4,32,256]{2,1,0:T(8,128)} copy(f32[4,32,256]{2,1,0:T(8,128)S(1)} %shard_map.37) | data formatting | bytes 262144

commit v4 on v3

--- a/solution.py
+++ b/solution.py
@@ -14,19 +14,23 @@
 
 
 def kernel(chol_hbm, orb_hbm, pairs_hbm, out_ref, chol_v, orb_v, pairs_s, acc, half_send, half_recv, orb_t,
-           part_send, part_recv, index_send, index_recv, rows_send, rows_recv,
+           part_send, part_sum, part_recv, index_send, index_recv, rows_send, rows_recv,
            load_sem, pairs_sem, half_sems, part_sems, index_sems, rows_sems):
     c, a = lax.axis_index("chol"), lax.axis_index("ao")
     quad, i = a >> 4, a & 15
-    flip = 12 * (quad >> 1)
-    block = i ^ flip
+
+    def turned(q, place):
+        far = q >> 1
+        return (((1 - 2 * far) * (place >> 2) + 3 * far * (1 - (q & 1))) & 3) * 4 + (place & 3)
+
+    block = turned(quad, i)
 
     def member(place):
         return quad * GROUP + place
 
     def same_block(d):
         other = (quad + d) & 3
-        return other * GROUP + (block ^ (12 * (other >> 1)))
+        return other * GROUP + turned(other, block)
 
     width = chol_v.shape[2] // CHUNKS
 
@@ -78,13 +82,17 @@
     index_send[0] = line
     index_recv[i] = line
 
+    @pl.when(quad == 1)
+    def _():
+        part_recv[1] = jnp.zeros((128, 128), BF16)
+
     pl.semaphore_wait(barrier, QUADS - 1 + GROUP - 1 + CHOL - 1)
 
     halves, indices = [], []
     for d in (10, 11, 9, 8, 14, 15, 13, 12, 6, 7, 5, 4, 2, 3, 1):
         to = (c, member(i ^ d))
         halves.append(pltpu.make_async_remote_copy(
-            half_send.at[block ^ d], half_recv.at[i], half_sems.at[0], half_sems.at[1], device_id=to, device_id_type=MESH))
+            half_send.at[turned(quad, i ^ d)], half_recv.at[i], half_sems.at[0], half_sems.at[1], device_id=to, device_id_type=MESH))
         indices.append(pltpu.make_async_remote_copy(
             index_send.at[0], index_recv.at[i], index_sems.at[0], index_sems.at[1], device_id=to, device_id_type=MESH))
     for copy in halves + indices:
@@ -108,13 +116,21 @@
     odd = jnp.dot(orb_t[1], rows, preferred_element_type=F32)
     own = jnp.where(lane(128) < 64, even[:128] + swap(odd[:128]), swap(even[128:]) + odd[128:])
     part_send[...] = own.astype(BF16)
-    parts = []
-    for d in (2, 1, 3):
-        copy = pltpu.make_async_remote_copy(
-            part_send, part_recv.at[d - 1], part_sems.at[0], part_sems.at[d],
+
+    def part(d, source):
+        return pltpu.make_async_remote_copy(
+            source, part_recv.at[d - 1], part_sems.at[0], part_sems.at[d],
             device_id=(c, same_block(d)), device_id_type=MESH)
-        copy.start()
-        parts.append(copy)
+
+    @pl.when(quad != 3)
+    def _():
+        part(2, part_send).start()
+
+    @pl.when(quad != 0)
+    def _():
+        part(1, part_send).start()
+
+    part(3, part_send).start()
     acc[:128, :128] = own
 
     wait_for(index_sems.at[1], index_recv.at[pl.ds(0, GROUP - 1)])
@@ -127,10 +143,21 @@
     ones = jnp.concatenate([hot(0, 0), hot(1, 0), hot(0, 1), hot(1, 1)], axis=0)
 
     total = acc[:128, :128]
-    for copy in parts:
-        copy.wait_recv()
-    for d in range(3):
-        total = total + part_recv[d].astype(F32)
+    part(1, part_send).wait_recv()
+    total = total + part_recv[0].astype(F32)
+
+    @pl.when(quad == 0)
+    def _():
+        part_sum[...] = total.astype(BF16)
+        part(1, part_sum).start()
+
+    part(3, part_send).wait_recv()
+
+    @pl.when(quad != 1)
+    def _():
+        part(2, part_send).wait_recv()
+
+    total = total + part_recv[1].astype(F32) + part_recv[2].astype(F32)
     chosen = jnp.dot(ones, total.astype(BF16), preferred_element_type=F32)
     message = jnp.where(
         lane(64) < 64, chosen[:64] + swap(chosen[128:192]), swap(chosen[64:128]) + chosen[192:256])
@@ -145,14 +172,19 @@
 
     def send_member(j, carry):
         for f in (4, 5, 6, 7, 2, 3, 0, 1):
-            send(i ^ (15 - j), f)
+            send(j + (j >= i).astype(jnp.int32), f)
         return carry
 
     lax.fori_loop(0, 15, send_member, 0)
     for f in (4, 5, 6, 7, 2, 3, 1):
         send(i, f)
-    for copy in parts:
-        copy.wait_send()
+    part(1, part_send).wait_send()
+    part(3, part_send).wait_send()
+
+    @pl.when(quad != 3)
+    def _():
+        part(2, part_send).wait_send()
+
     for copy in indices:
         copy.wait_send()
     wait_for(half_sems.at[0], half_recv.at[pl.ds(0, GROUP - 1)])
@@ -164,10 +196,9 @@
     for t in range(4):
         moved = left if t == 0 else pltpu.roll(left, 32 * t, axis=1)
         wide = jnp.where((row(128) % 4 == t) & (lane(128) // 32 == t), moved, wide)
-    wide = wide.astype(BF16)
+    wide = wide.T.astype(BF16)
     products = [
-        lax.dot_general(wide, rows_recv[z * 32 : z * 32 + 32].reshape(128, 128),
-                        (((0,), (0,)), ((), ())), preferred_element_type=F32)
+        jnp.dot(wide, rows_recv[z * 32 : z * 32 + 32].reshape(128, 128), preferred_element_type=F32)
         for z in range(4)
     ]
     for h in range(2):
@@ -191,6 +222,7 @@
             vmem((16, 32, 128), BF16),
             vmem((16, 32, 128), BF16),
             vmem((2, 256, 512), BF16),
+            vmem((128, 128), BF16),
             vmem((128, 128), BF16),
             vmem((3, 128, 128), BF16),
             vmem((1, 1, 128), F32),

time: 38 us -> 37.3 us (0.982)
  Pallas kernels: 37.2 us -> 36.5 us
    pallas_call x1, Pallas kernels: 37.2 us -> 36.5 us  [on_device(): pl.pallas_call(kernel, out_shape=jax.ShapeDtypeStruct((4, 32, 256), F32),...]
where the time goes in v4:
time: 37.3 us; the launch traced here: 37.2 us
  Pallas kernels  36.5 us (98%)
  local copies, waits for them, and re-layouts  0.66 us (2%)
    pallas_call x1, Pallas kernels, on_device(): pl.pallas_call(kernel, out_shape=jax.ShapeDtypeStruct((4, 32, 256), F32),...  36.5 us

profile of v4, /device:TPU:1, one launch (start us, length us, event | category | flops | bytes accessed | tf_op | source)
XLA Modules:
  0.0 37.2 jit_solution(8121737881479224629)
XLA Ops:
  0.0 36.5 %shard_map.37 = f32[4,32,256]{2,1,0:T(8,128)S(1)} custom-call(bf16[4,64,4096]{2,1,0:T(8,128)(2,1)} %chol_hbm.1, bf16[4096,256]{1,0:T(8,128)(2,1)} %orb_hbm.1, s32[1,2,4]{2,1,0:T(2,128)} %bitcast.1), custom_call_target="tpu_custom_call" | custom-call | flops 700000000 | bytes 4400000 | tf_op jit(solution)/shard_map/pallas_call | solution.py:212
  36.5 0.7 %copy.5 = f32[4,32,256]{2,1,0:T(8,128)} copy(f32[4,32,256]{2,1,0:T(8,128)S(1)} %shard_map.37) | data formatting | bytes 262144
